TPU v7x, 128 devices: a whole 4x4x4 slice. The times are simulated.
128 devices in a mesh: rows: 4 (over y_hi, core), loop: 32 (over z, x, y_lo).
Axes of the slice: x: 4, y: 4 (y_hi: 2, y_lo: 2; y = y_hi * 2 + y_lo), z: 4, core: 2. Of those that a mesh axis runs over, the one named last changes fastest.
Arguments:
- delta_weight_matrix: float32 [98304, 4096], P('rows', 'loop'), may hold values from -18 to 18
- offsets: int32 [2, 4], replicated, may hold values from 0 to 63, as said below
Outputs:
- rotated: float32 [98304, 4096], P('rows', 'loop')
Inputs may be any that keep to these rules, and one draw needn't show every extreme that they name: The 4 offsets of each step are distinct.
All inputs are finite; a program needn't handle non-finite values.
Results may differ from a plain program's by a relative error of at most 0.0003.
Values sent between devices are 32-bit elements; how exact they have to be, the bound alone decides.
No kernel may reach another device: no remote copies, remote signals or barrier semaphores. Data moves between devices by JAX's collectives and lax.ppermute only.
A program may use at most 128 MiB of HBM per device.

v0:
```python
import jax
import jax.numpy as jnp
from jax import lax
from jax.sharding import PartitionSpec as P

INNER_ROUNDS = 4
PRECISION_HIGH = lax.Precision.HIGHEST


def passed_along(shard, axis, by):
    devices = lax.axis_size(axis)
    pairs = [(i, i + by) for i in range(devices) if 0 <= i + by < devices]
    return lax.ppermute(shard, axis, pairs)


def paired_gram_matrix(left, right):
    return lax.dot_general(
        left,
        right,
        (((0,), (0,)), ((), ())),
        precision=PRECISION_HIGH,
        preferred_element_type=jnp.float32,
    )


def jacobi_rotations(gram_matrix, circle_shifts):
    block_width = gram_matrix.shape[0]
    half = block_width // 2
    right_vectors = jnp.eye(block_width, dtype=gram_matrix.dtype)
    column = jnp.arange(half, dtype=jnp.int32)
    for which in range(INNER_ROUNDS):
        partner = half + (column + circle_shifts[which]) % half
        g_first = gram_matrix[column, column]
        g_second = gram_matrix[partner, partner]
        g_cross = gram_matrix[column, partner]
        spread = g_second - g_first
        sign_part = jnp.where(spread >= 0.0, 1.0, -1.0).astype(gram_matrix.dtype)
        tangent = (
            sign_part
            * 2.0
            * g_cross
            / (jnp.abs(spread) + jnp.sqrt(spread * spread + 4.0 * g_cross * g_cross))
        )
        cosine = 1.0 / jnp.sqrt(1.0 + tangent * tangent)
        sine = -tangent * cosine
        rotate_pair = jnp.zeros((block_width, block_width), gram_matrix.dtype)
        rotate_pair = rotate_pair.at[column, column].set(cosine).at[partner, partner].set(cosine)
        rotate_pair = rotate_pair.at[partner, column].set(sine).at[column, partner].set(-sine)
        gram_matrix = jnp.dot(
            rotate_pair.T,
            jnp.dot(gram_matrix, rotate_pair, precision=PRECISION_HIGH),
            precision=PRECISION_HIGH,
        )
        right_vectors = jnp.dot(right_vectors, rotate_pair, precision=PRECISION_HIGH)
    return (right_vectors, gram_matrix)


def reduced_gram_matrix(column_block):
    return lax.psum(paired_gram_matrix(column_block, column_block), "rows")


def body(delta_weight_matrix, offsets):
    half = delta_weight_matrix.shape[1] // 2
    place = lax.axis_index("loop")
    count = lax.axis_size("loop")
    first_place = place == 0
    last_place = place == count - 1
    right_vectors, rotated_blocks = jacobi_rotations(
        reduced_gram_matrix(delta_weight_matrix), offsets[0]
    )
    advanced_blocks = jnp.dot(
        delta_weight_matrix,
        right_vectors,
        precision=PRECISION_HIGH,
        preferred_element_type=jnp.float32,
    )
    first_half = advanced_blocks[:, :half]
    second_half = advanced_blocks[:, half:]
    arrived_up = passed_along(jnp.where(first_place, second_half, first_half), "loop", 1)
    arrived_down = passed_along(second_half, "loop", -1)
    new_first = jnp.where(first_place, first_half, arrived_up)
    new_second = jnp.where(last_place, first_half, arrived_down)
    shifted_blocks = jnp.concatenate([new_first, new_second], 1)
    updated_gram_matrix = reduced_gram_matrix(shifted_blocks)
    updated_right_vectors, discarded_value = jacobi_rotations(updated_gram_matrix, offsets[1])
    return jnp.dot(
        shifted_blocks,
        updated_right_vectors,
        precision=PRECISION_HIGH,
        preferred_element_type=jnp.float32,
    )


def solution(mesh):
    placed = (P("rows", "loop"), P())
    return jax.shard_map(
        body, mesh=mesh, in_specs=placed, out_specs=P("rows", "loop"), check_vma=False
    )
```

profile of v0, /device:TPU:1, one launch (start us, length us, event | category | flops | bytes accessed | tf_op | source)
XLA Modules:
  0.0 632.7 jit_solution(15431990333249425547)
XLA Ops:
  6.5 28.9 %fusion.116 = f32[128,128]{1,0:T(8,128)} fusion(f32[24576,128]{1,0:T(8,128)} %param.2), kind=kOutput, calls=%fused_computation.285 | convolution fusion | flops 4831838208 | bytes 12648448 | tf_op jit(solution)/shard_map/dot_general | solution.py:17
  43.9 35.2 %all-reduce.3.cloned.1.call-done = f32[128,128]{1,0:T(8,128)} async-done(((f32[128,128]{1,0:T(8,128)}), f32[128,128]{1,0:T(8,128)}) %all-reduce.3.cloned.1.call-update) | async-done | bytes 65552 | tf_op jit(solution)/shard_map/psum | solution.py:59
  84.2 4.0 scatter_fusion
  95.8 3.8 scatter_fusion.3
  103.5 3.8 scatter_fusion.4
  114.9 3.8 scatter_fusion.7
  121.6 3.8 scatter_fusion.8
  125.4 3.8 scatter_fusion.9
  129.2 3.8 scatter_fusion.10
  133.0 4.2 scatter_fusion.11
  140.6 3.8 scatter_fusion.12
  151.9 3.8 scatter_fusion.15
  156.0 17.3 %convolution_bitcast_fusion = f32[24576,128]{0,1:T(8,128)} fusion(f32[128,128]{1,0:T(8,128)S(1)} %fusion.125, f32[24576,128]{1,0:T(8,128)} %param.2), kind=kOutput, calls=%fused_computation.56 | convolution fusion | flops 4831838208 | bytes 25231360 | tf_op jit(solution)/shard_map/dot_general | solution.py:71
  173.2 10.4 %slice_select_fusion.2 = (f32[24576,64]{0,1:T(8,128)}, f32[24576,64]{0,1:T(8,128)}) fusion(f32[24576,128]{0,1:T(8,128)} %convolution_bitcast_fusion, pred[]{:T(512)S(6)} %eq.21), kind=kLoop, calls=%fused_computation.62 | loop fusion | flops 1572864 | bytes 25165824 | tf_op jit(solution)/shard_map/jit(_where)/select_n | solution.py:79
  183.6 4.9 collective-permute-start
  196.5 259.1 %collective-permute-done = f32[24576,64]{0,1:T(8,128)} collective-permute-done((f32[24576,64]{0,1:T(8,128)}, f32[24576,64]{0,1:T(8,128)}, u32[]{:S(2)}, u32[]{:S(2)}) %collective-permute-start) | collective-permute-done | bytes 6291488 | tf_op jit(solution)/shard_map/ppermute | solution.py:13
  455.7 5.5 collective-permute-done.1
  461.2 10.4 %slice_select_fusion.1 = (f32[24576,64]{0,1:T(8,128)}, f32[24576,64]{0,1:T(8,128)}) fusion(f32[24576,64]{0,1:T(8,128)} %collective-permute-done, f32[24576,128]{0,1:T(8,128)} %convolution_bitcast_fusion, pred[]{:T(512)S(6)} %eq.21, f32[24576,64]{0,1:T(8,128)} %collective-permute-done.1, pred[]{:T(512)S(6)} %eq.23), kind=kLoop, calls=%fused_computation.61 | loop fusion | flops 3145728 | bytes 31457282 | tf_op jit(solution)/shard_map/jit(_where)/select_n | solution.py:81
  471.5 14.8 %fusion.1 = f32[128,128]{1,0:T(8,128)} fusion(f32[24576,64]{0,1:T(8,128)} %get-tuple-element.30, f32[24576,64]{0,1:T(8,128)} %get-tuple-element.29), kind=kOutput, calls=%fused_computation.59 | convolution fusion | flops 4834983936 | bytes 12648448 | tf_op jit(solution)/shard_map/dot_general | solution.py:17
  487.0 37.9 %all-reduce.5.cloned.1.call-done = f32[128,128]{1,0:T(8,128)} async-done(((f32[128,128]{1,0:T(8,128)}), f32[128,128]{1,0:T(8,128)}) %all-reduce.5.cloned.1.call-update) | async-done | bytes 65552 | tf_op jit(solution)/shard_map/psum | solution.py:59
  530.1 3.8 scatter_fusion.16
  541.4 3.8 scatter_fusion.19
  560.5 4.0 scatter_fusion.23
  601.3 24.1 %fusion = f32[24576,128]{1,0:T(8,128)} fusion(f32[128,128]{1,0:T(8,128)S(1)} %fusion.134, f32[24576,64]{0,1:T(8,128)} %get-tuple-element.30, f32[24576,64]{0,1:T(8,128)} %get-tuple-element.29), kind=kOutput, calls=%fused_computation.58 | convolution fusion | flops 4834983936 | bytes 25231360 | tf_op jit(solution)/shard_map/dot_general | solution.py:86
  (121 shorter events, 119.7 us)
Async XLA Ops:
  6.5 29.0 %copy-start = (s32[2,4]{1,0:T(2,128)S(1)}, s32[2,4]{1,0:T(2,128)}, u32[]{:S(2)}) copy-start(s32[2,4]{1,0:T(2,128)} %param.3) | copy-start | bytes 100
  6.5 72.5 %all-reduce.3.cloned.1.call-start = ((), (), s32[]{:S(2)}) async-start(), calls=%async_computation | async-start | bytes 131072 | tf_op jit(solution)/shard_map/psum | solution.py:59
  35.4 489.5 %all-reduce.5.cloned.1.call-start = ((), (), s32[]{:S(2)}) async-start(), calls=%async_computation.1 | async-start | bytes 131072 | tf_op jit(solution)/shard_map/psum | solution.py:59
  183.6 272.1 %collective-permute-start = (f32[24576,64]{0,1:T(8,128)}, f32[24576,64]{0,1:T(8,128)}, u32[]{:S(2)}, u32[]{:S(2)}) collective-permute-start(f32[24576,64]{0,1:T(8,128)} %get-tuple-element.31), channel_id=1, source_target_pairs={{0,1},{1,2},{2,3},{3,4},{4,5},{5,6},{6,7},{7,8},{8,9},{9,10},{10,1... | collective-permute-start | bytes 18874376 | tf_op jit(solution)/shard_map/ppermute | solution.py:13
  188.5 272.7 %collective-permute-start.1 = (f32[24576,64]{0,1:T(8,128)}, f32[24576,64]{0,1:T(8,128)}, u32[]{:S(2)}, u32[]{:S(2)}) collective-permute-start(f32[24576,64]{0,1:T(8,128)} %get-tuple-element.32), channel_id=1, source_target_pairs={{1,0},{2,1},{3,2},{4,3},{5,4},{6,5},{7,6},{8,7},{9,8},{10,9},{11,1... | collective-permute-start | bytes 18874376 | tf_op jit(solution)/shard_map/ppermute | solution.py:13
Sparse Core Ops, SparseCore 0:
  35.6 43.4 all-reduce.2
  486.5 38.4 all-reduce.4
where the time goes:
time: 642 us; the launch traced here: 633 us
  waiting for transfers between devices  338 us (53%)
  local copies, waits for them, and re-layouts  147 us (23%)
  matrix products  91.2 us (14%)
  other arithmetic  35.9 us (6%)
  between operations  14.5 us (2%)
    ppermute x2, waiting for transfers between devices, passed_along(): return lax.ppermute(shard, axis, pairs)  265 us
    psum x2, waiting for transfers between devices, reduced_gram_matrix(): return lax.psum(paired_gram_matrix(column_block, column_block), 'rows')  73.1 us
    scatter x16, local copies, waits for them, and re-layouts, jacobi_rotations(): rotate_pair.at[partner, column].set(sine).at[column, partner].set(-sine)  61.2 us
    scatter x16, local copies, waits for them, and re-layouts, jacobi_rotations(): rotate_pair.at[column, column].set(cosine).at[partner, partner].set(cosine)  60.7 us
    dot_general x2, matrix products, paired_gram_matrix(): lax.dot_general(left, right, (((0,), (0,)), ((), ())), precision=PRECISIO...  43.7 us
    dot_general x1, matrix products, body(): jnp.dot(shifted_blocks, updated_right_vectors, precision=PRECISION_HIGH,...  24.1 us
    dot_general x1, matrix products, body(): jnp.dot(delta_weight_matrix, right_vectors, precision=PRECISION_HIGH, pre...  17.3 us
  transfers between devices with their start and end apart: 4, of which 4 were waited for; matrix products, arithmetic and copies ran while one was open for 2% of the time, Pallas kernels for 0%

commit v1 on v0

--- a/solution.py
+++ b/solution.py
@@ -56,7 +56,9 @@
 
 
 def reduced_gram_matrix(column_block):
-    return lax.psum(paired_gram_matrix(column_block, column_block), "rows")
+    return jnp.sum(
+        jax.lax.all_gather(paired_gram_matrix(column_block, column_block), "rows"), axis=0
+    )
 
 
 def body(delta_weight_matrix, offsets):

time: 642 us -> 564 us (0.88)
  waiting for transfers between devices: 338 us -> 263 us
  blocking collectives: 0 us -> 16.4 us
  between operations: 14.5 us -> 1.08 us
    psum x2 -> x0, waiting for transfers between devices: 73.1 us -> none  [reduced_gram_matrix(): return lax.psum(paired_gram_matrix(column_block, column_block), 'rows')]
    all_gather x0 -> x2, blocking collectives: none -> 16.4 us  [reduced_gram_matrix(): jax.lax.all_gather(paired_gram_matrix(column_block, column_block), 'rows')]
  transfers between devices with their start and end apart: 4 -> 2, of which waited for: 4 -> 2; matrix products, arithmetic and copies ran while one was open for 2% -> 1% of each run, Pallas kernels for 0% -> 0%
where the time goes in v1:
time: 564 us; the launch traced here: 555 us
  waiting for transfers between devices  263 us (47%)
  local copies, waits for them, and re-layouts  143 us (25%)
  matrix products  87.9 us (16%)
  other arithmetic  36.1 us (6%)
  blocking collectives  16.4 us (3%)
  starting transfers between devices  7.16 us (1%)
    ppermute x2, waiting for transfers between devices, passed_along(): return lax.ppermute(shard, axis, pairs)  263 us
    scatter x16, local copies, waits for them, and re-layouts, jacobi_rotations(): rotate_pair.at[partner, column].set(sine).at[column, partner].set(-sine)  61.2 us
    scatter x16, local copies, waits for them, and re-layouts, jacobi_rotations(): rotate_pair.at[column, column].set(cosine).at[partner, partner].set(cosine)  60.8 us
    dot_general x2, matrix products, paired_gram_matrix(): lax.dot_general(left, right, (((0,), (0,)), ((), ())), precision=PRECISIO...  42.3 us
    dot_general x1, matrix products, body(): jnp.dot(shifted_blocks, updated_right_vectors, precision=PRECISION_HIGH,...  23.8 us
    dot_general x1, matrix products, body(): jnp.dot(delta_weight_matrix, right_vectors, precision=PRECISION_HIGH, pre...  17.3 us
    all_gather x2, blocking collectives, reduced_gram_matrix(): jax.lax.all_gather(paired_gram_matrix(column_block, column_block), 'rows')  16.4 us
  transfers between devices with their start and end apart: 2, of which 2 were waited for; matrix products, arithmetic and copies ran while one was open for 1% of the time, Pallas kernels for 0%

profile of v1, /device:TPU:1, one launch (start us, length us, event | category | flops | bytes accessed | tf_op | source)
XLA Modules:
  0.0 554.7 jit_solution(15955554952179478274)
XLA Ops:
  9.5 28.3 %fusion.116 = f32[128,128]{1,0:T(8,128)S(1)} fusion(f32[24576,128]{1,0:T(8,128)} %param.2), kind=kOutput, calls=%fused_computation.285 | convolution fusion | flops 4831838208 | bytes 12648448 | tf_op jit(solution)/shard_map/dot_general | solution.py:17
  37.8 8.8 %all-gather = f32[512,128]{1,0:T(8,128)S(1)} all-gather(f32[128,128]{1,0:T(8,128)S(1)} %fusion.116), channel_id=2, replica_groups=mesh['rows'=4,'loop'=32] {'rows'}, dimensions={0}, use_global_device_ids=true | all-gather | bytes 327680 | tf_op jit(solution)/shard_map/all_gather | solution.py:60
  49.0 4.0 scatter_fusion
  60.6 3.8 scatter_fusion.3
  67.5 3.8 scatter_fusion.4
  78.9 3.8 scatter_fusion.7
  85.6 3.8 scatter_fusion.8
  89.4 3.8 scatter_fusion.9
  93.2 3.8 scatter_fusion.10
  97.0 4.3 scatter_fusion.11
  104.6 3.8 scatter_fusion.12
  116.0 3.8 scatter_fusion.15
  120.0 17.3 %convolution_bitcast_fusion = f32[24576,128]{0,1:T(8,128)} fusion(f32[128,128]{1,0:T(8,128)S(1)} %fusion.125, f32[24576,128]{1,0:T(8,128)} %param.2), kind=kOutput, calls=%fused_computation.56 | convolution fusion | flops 4831838208 | bytes 25231360 | tf_op jit(solution)/shard_map/dot_general | solution.py:73
  137.3 10.4 %slice_select_fusion.2 = (f32[24576,64]{0,1:T(8,128)}, f32[24576,64]{0,1:T(8,128)}) fusion(f32[24576,128]{0,1:T(8,128)} %convolution_bitcast_fusion, pred[]{:T(512)S(6)} %eq.21), kind=kLoop, calls=%fused_computation.62 | loop fusion | flops 1572864 | bytes 25165824 | tf_op jit(solution)/shard_map/jit(_where)/select_n | solution.py:81
  147.6 5.7 %collective-permute-start = (f32[24576,64]{0,1:T(8,128)}, f32[24576,64]{0,1:T(8,128)}, u32[]{:S(2)}, u32[]{:S(2)}) collective-permute-start(f32[24576,64]{0,1:T(8,128)} %get-tuple-element.31), channel_id=1, source_target_pairs={{0,1},{1,2},{2,3},{3,4},{4,5},{5,6},{6,7},{7,8},{8,9},{9,10},{10,1... | collective-permute-start | bytes 18874376 | tf_op jit(solution)/shard_map/ppermute | solution.py:13
  162.2 258.3 %collective-permute-done = f32[24576,64]{0,1:T(8,128)} collective-permute-done((f32[24576,64]{0,1:T(8,128)}, f32[24576,64]{0,1:T(8,128)}, u32[]{:S(2)}, u32[]{:S(2)}) %collective-permute-start) | collective-permute-done | bytes 6291488 | tf_op jit(solution)/shard_map/ppermute | solution.py:13
  420.6 5.0 collective-permute-done.1
  425.6 10.4 %slice_select_fusion.1 = (f32[24576,64]{0,1:T(8,128)}, f32[24576,64]{0,1:T(8,128)}) fusion(f32[24576,64]{0,1:T(8,128)} %collective-permute-done, f32[24576,128]{0,1:T(8,128)} %convolution_bitcast_fusion, pred[]{:T(512)S(6)} %eq.21, f32[24576,64]{0,1:T(8,128)} %collective-permute-done.1, pred[]{:T(512)S(6)} %eq.23), kind=kLoop, calls=%fused_computation.61 | loop fusion | flops 3145728 | bytes 31457282 | tf_op jit(solution)/shard_map/jit(_where)/select_n | solution.py:83
  435.9 14.0 %fusion.1 = f32[128,128]{1,0:T(8,128)S(1)} fusion(f32[24576,64]{0,1:T(8,128)} %get-tuple-element.30, f32[24576,64]{0,1:T(8,128)} %get-tuple-element.29), kind=kOutput, calls=%fused_computation.59 | convolution fusion | flops 4834983936 | bytes 12648448 | tf_op jit(solution)/shard_map/dot_general | solution.py:17
  450.0 7.6 %all-gather.1 = f32[512,128]{1,0:T(8,128)S(1)} all-gather(f32[128,128]{1,0:T(8,128)S(1)} %fusion.1), channel_id=3, replica_groups=mesh['rows'=4,'loop'=32] {'rows'}, dimensions={0}, use_global_device_ids=true | all-gather | bytes 327680 | tf_op jit(solution)/shard_map/all_gather | solution.py:60
  460.0 3.8 scatter_fusion.16
  471.4 3.8 scatter_fusion.19
  507.7 4.0 scatter_fusion.27
  530.5 23.8 %fusion = f32[24576,128]{1,0:T(8,128)} fusion(f32[128,128]{1,0:T(8,128)S(1)} %fusion.134, f32[24576,64]{0,1:T(8,128)} %get-tuple-element.30, f32[24576,64]{0,1:T(8,128)} %get-tuple-element.29), kind=kOutput, calls=%fused_computation.58 | convolution fusion | flops 4834983936 | bytes 25231360 | tf_op jit(solution)/shard_map/dot_general | solution.py:88
  (117 shorter events, 113.9 us)
Async XLA Ops:
  147.6 272.9 %collective-permute-start = (f32[24576,64]{0,1:T(8,128)}, f32[24576,64]{0,1:T(8,128)}, u32[]{:S(2)}, u32[]{:S(2)}) collective-permute-start(f32[24576,64]{0,1:T(8,128)} %get-tuple-element.31), channel_id=1, source_target_pairs={{0,1},{1,2},{2,3},{3,4},{4,5},{5,6},{6,7},{7,8},{8,9},{9,10},{10,1... | collective-permute-start | bytes 18874376 | tf_op jit(solution)/shard_map/ppermute | solution.py:13
  153.3 272.2 %collective-permute-start.1 = (f32[24576,64]{0,1:T(8,128)}, f32[24576,64]{0,1:T(8,128)}, u32[]{:S(2)}, u32[]{:S(2)}) collective-permute-start(f32[24576,64]{0,1:T(8,128)} %get-tuple-element.32), channel_id=1, source_target_pairs={{1,0},{2,1},{3,2},{4,3},{5,4},{6,5},{7,6},{8,7},{9,8},{10,9},{11,1... | collective-permute-start | bytes 18874376 | tf_op jit(solution)/shard_map/ppermute | solution.py:13
